TPU v7x, 256 devices: a whole 4x4x8 slice. The times are simulated.
256 devices in a mesh: grp: 16 (over z, core), tp: 16 (over y, x).
Axes of the slice: x: 4, y: 4, z: 8, core: 2. Of those that a mesh axis runs over, the one named last changes fastest.
Arguments:
- tensor_blocks: bfloat16 [256, 3, 128, 64, 128], P(('grp', 'tp')), may hold values from -6 to 6
- occupied: bfloat16 [256, 3, 128, 128], P('grp'), may hold values from -0.3125 to 0.3125
- virtual: bfloat16 [256, 3, 128, 128], P('grp'), may hold values from -0.3125 to 0.3125
- slot_block: int32 [16, 16], P('grp'), may hold values from 0 to 15, each once within a row
- pair_kept: int32 [256], replicated, may hold values 0 or 1
- block_funcs: int32 [256], replicated, may hold values from 96 to 128
Outputs:
- polarizability: float32 [256, 5, 64, 64], P(('grp', 'tp'))
Inputs may be any that keep to these rules, and one draw needn't show every extreme that they name: `slot_block`: each row is a permutation of the region's 16 columns. `pair_kept`: entry j filters the pair of AO blocks j and j + 1 (both orders). `block_funcs`: functions past this count in a block of 128 are padding.
All inputs are finite; a program needn't handle non-finite values.
Results may differ from a plain program's by a relative error of at most 0.0041.
Values may be sent and summed in bfloat16 or wider, within the bound.
A program may use at most 128 MiB of HBM per device.

v0:
```python
import jax
import jax.numpy as jnp
from jax import lax
from jax.experimental import pallas as pl
from jax.experimental.pallas import tpu as pltpu
from jax.sharding import PartitionSpec as P

MESH = pl.DeviceIdType.MESH
BF = jnp.bfloat16
F32 = jnp.float32
SIDE = 4

NEAR = [(dx, dy) for dy in (-1, 0, 1) for dx in (-1, 0, 1) if (dx, dy) != (0, 0)]
FAR = [(2, 0), (0, 2), (2, 1), (2, -1), (1, 2), (-1, 2), (2, 2)]
RELAY = []
for _dx, _dy in FAR:
    for _half, _sign in enumerate((1, -1)):
        _first = (_sign if _dx == 2 else _dx, _sign if _dy == 2 else _dy)
        RELAY.append((_first, (_dx - _first[0], _dy - _first[1]), _half))
ALL = NEAR + FAR


def place(dx, dy):
    me = lax.axis_index("tp")
    x = lax.rem(lax.rem(me, SIDE) + (dx + SIDE), SIDE)
    y = lax.rem(me // SIDE + (dy + SIDE), SIDE)
    return y * SIDE + x


def slice_of(tp):
    x, y = lax.rem(tp, SIDE), tp // SIDE
    return y * 2 + x // 2, lax.rem(x + y, 2)


def lanes(x):
    return jnp.concatenate([x[i] for i in range(x.shape[0])], axis=1)


def dot_nt(a, b):
    return lax.dot_general(a, b, (((1,), (1,)), ((), ())), preferred_element_type=F32)


def kernel(
    inv, kt, ot, vd, vv, out,
    kh, k32, h32, r01, r2, rb, zd, zu, ed, eu, es, pt, fin, dg, acc,
    near_s, near_r, one_s, one_r, two_s, two_r, edge_s, edge_r, fin_s, fin_r, dg_s, dg_r, loc,
):
    me = lax.axis_index("tp")
    grp = lax.axis_index("grp")
    regions = lax.axis_size("grp")
    rows = 16
    kind = slice_of(me)[1]

    def dev(dx, dy):
        return (grp, place(dx, dy))

    def grp_at(step):
        return (lax.rem(grp + step + regions, regions), me)

    load = pltpu.make_async_copy(kt, kh.at[pl.ds(0, 3)], loc.at[3])
    load.start()

    barrier = pltpu.get_barrier_semaphore()
    for dx, dy in ALL:
        pl.semaphore_signal(barrier, inc=1, device_id=dev(dx, dy), device_id_type=MESH)
    for step in (1, -1):
        pl.semaphore_signal(barrier, inc=1, device_id=grp_at(step), device_id_type=MESH)
    pl.semaphore_wait(barrier, len(ALL) + 2)

    def landing(slot, origin):
        return r2.at[origin] if slot == 2 else r01.at[slot, origin]

    def source(slot, target, start, count):
        u, v = slice_of(target)
        part = pl.ds(u * rows + start, count)
        if slot == 0:
            return kt.at[v, part]
        which = 2 + 3 * v if slot == 1 else 4 - v
        return kh.at[which, part]

    copies = []

    def send(slot):
        firsts = []
        for i, (first, second, half) in enumerate(RELAY):
            target = place(first[0] + second[0], first[1] + second[1])
            c = pltpu.make_async_remote_copy(
                src_ref=source(slot, target, half * 8, 8),
                dst_ref=rb.at[slot, i],
                send_sem=one_s.at[slot, i],
                recv_sem=one_r.at[slot, i],
                device_id=dev(*first),
                device_id_type=MESH,
            )
            c.start()
            firsts.append(c)
        nears = []
        for i, (dx, dy) in enumerate(NEAR):
            c = pltpu.make_async_remote_copy(
                src_ref=source(slot, place(dx, dy), 0, rows),
                dst_ref=landing(slot, me),
                send_sem=near_s.at[slot, i],
                recv_sem=near_r.at[slot, i],
                device_id=dev(dx, dy),
                device_id_type=MESH,
            )
            c.start()
            nears.append(c)
        own = pltpu.make_async_copy(source(slot, me, 0, rows), landing(slot, me), loc.at[slot])
        own.start()
        return firsts, nears, own

    def forward(slot, firsts):
        seconds = []
        for i, (first, second, half) in enumerate(RELAY):
            firsts[i].wait_recv()
            c = pltpu.make_async_remote_copy(
                src_ref=rb.at[slot, i],
                dst_ref=landing(slot, place(-first[0], -first[1])).at[pl.ds(half * 8, 8)],
                send_sem=two_s.at[slot, i],
                recv_sem=two_r.at[slot, i],
                device_id=dev(*second),
                device_id_type=MESH,
            )
            c.start()
            seconds.append(c)
        return seconds

    def arrive(nears, own, seconds):
        own.wait()
        for c in nears + seconds:
            c.wait_recv()

    firsts0, nears0, own0 = send(0)
    load.wait()

    def half_chunk(i, _):
        cut = pl.ds(pl.multiple_of(i * 16, 16), 16)
        for d in range(3):
            k32[pl.ds(d * 2048, 2048), :] = kh[d, :, cut, :].reshape(2048, 128).astype(F32)
        for q in range(0, 16, 2):
            two = [k32[pl.ds(q + s, 384, stride=16), :] for s in range(2)]
            res = jnp.dot(
                ot[...], jnp.concatenate(two, axis=1).astype(BF), preferred_element_type=F32
            )
            for s in range(2):
                h32[pl.ds(q + s, 384, stride=16), :] = res[:, s * 128 : (s + 1) * 128]
        for e in range(3):
            kh[3 + e, :, cut, :] = h32[pl.ds(e * 2048, 2048), :].reshape(128, 16, 128).astype(BF)
        return 0

    lax.fori_loop(0, 4, half_chunk, 0)

    firsts1, nears1, own1 = send(1)
    seconds0 = forward(0, firsts0)
    firsts2, nears2, own2 = send(2)

    acc[...] = jnp.zeros_like(acc)

    def own_part(i, _):
        e, cut = i // 8, pl.ds(lax.rem(i, 8) * 16, 16)
        z = jnp.dot(kh[e, cut].reshape(1024, 128), vd[e], preferred_element_type=F32)
        acc[...] += dot_nt(lanes(kh[3 + e, cut]), lanes(z.astype(BF).reshape(16, 64, 128)))
        return 0

    seconds1 = forward(1, firsts1)
    lax.fori_loop(0, 24, own_part, 0)
    dg[me] = jnp.concatenate([acc[:32], acc[32:]], axis=1)
    shares = []
    for i, (dx, dy) in enumerate(ALL):
        c = pltpu.make_async_remote_copy(
            src_ref=dg.at[me],
            dst_ref=dg.at[me],
            send_sem=dg_s.at[i],
            recv_sem=dg_r.at[i],
            device_id=dev(dx, dy),
            device_id_type=MESH,
        )
        c.start()
        shares.append(c)

    seconds2 = forward(2, firsts2)

    arrive(nears0, own0, seconds0)
    arrive(nears1, own1, seconds1)

    es[0] = r01[0, inv[0]]
    es[1] = r01[1 - kind, inv[15]]
    edges = []
    for i, (step, dst) in enumerate(((-1, ed), (1, eu))):
        c = pltpu.make_async_remote_copy(
            src_ref=es.at[i],
            dst_ref=dst,
            send_sem=edge_s.at[i],
            recv_sem=edge_r.at[i],
            device_id=grp_at(step),
            device_id_type=MESH,
        )
        c.start()
        edges.append(c)

    def times(block, v):
        z = jnp.dot(block.reshape(1024, 128), v, preferred_element_type=F32)
        return z.astype(BF).reshape(16, 64, 128)

    def other_part(j, _):
        zd[j] = times(r01[0, inv[j + 1]], vv[j, 1])
        zu[j + 1] = times(r01[1 - kind, inv[j]], vv[j + 1, 0])
        return 0

    lax.fori_loop(0, 15, other_part, 0)
    for c in edges:
        c.wait_recv()
    zd[15] = times(ed[...], vv[15, 1])
    zu[0] = times(eu[...], vv[0, 0])

    arrive(nears2, own2, seconds2)

    @pl.when(kind == 0)
    def _():
        def part(j, _):
            half = lanes(r2[inv[j]])
            pt[j] = jnp.concatenate([dot_nt(half, lanes(zu[j])), dot_nt(half, lanes(zd[j]))], axis=1)
            return 0

        lax.fori_loop(0, 16, part, 0)

    @pl.when(kind == 1)
    def _():
        def part(j, _):
            pt[j] = jnp.concatenate(
                [
                    dot_nt(lanes(r2[inv[j]]), lanes(zu[j])),
                    dot_nt(lanes(r01[1, inv[j]]), lanes(zd[j])),
                ],
                axis=1,
            )
            return 0

        lax.fori_loop(0, 16, part, 0)

    sums = []
    for i, (dx, dy) in enumerate(ALL):
        c = pltpu.make_async_remote_copy(
            src_ref=pt.at[place(dx, dy)],
            dst_ref=fin.at[me],
            send_sem=fin_s.at[i],
            recv_sem=fin_r.at[i],
            device_id=dev(dx, dy),
            device_id_type=MESH,
        )
        c.start()
        sums.append(c)
    fin[me] = pt[me]
    for c in shares + sums:
        c.wait_recv()
    scale = 1.0 / 128
    total = fin[0]
    for k in range(1, 16):
        total = total + fin[k]
    total = total * scale
    mid = dg[inv[me]] * scale
    out[0] = jnp.zeros((64, 64), F32)
    out[1] = total[:, :64]
    out[2] = jnp.concatenate([mid[:, :64], mid[:, 64:]], axis=0)
    out[3] = total[:, 64:]
    out[4] = jnp.zeros((64, 64), F32)

    for c in firsts0 + firsts1 + firsts2 + nears0 + nears1 + nears2:
        c.wait_send()
    for c in seconds0 + seconds1 + seconds2 + edges + shares + sums:
        c.wait_send()


def fused(inv, kt, ot, vd, vv):
    dma = pltpu.SemaphoreType.DMA
    vmem = pl.BlockSpec(memory_space=pltpu.VMEM)
    near, far, every = len(NEAR), len(RELAY), len(ALL)
    return pl.pallas_call(
        kernel,
        out_shape=jax.ShapeDtypeStruct((5, 64, 64), F32),
        in_specs=[
            pl.BlockSpec(memory_space=pltpu.SMEM),
            pl.BlockSpec(memory_space=pl.ANY),
            vmem,
            vmem,
            vmem,
        ],
        out_specs=vmem,
        scratch_shapes=[
            pltpu.VMEM((6, 128, 64, 128), BF),
            pltpu.VMEM((6144, 128), F32),
            pltpu.VMEM((6144, 128), F32),
            pltpu.VMEM((2, 16, 16, 64, 128), BF),
            pltpu.VMEM((16, 16, 64, 128), BF),
            pltpu.VMEM((3, far, 8, 64, 128), BF),
            pltpu.VMEM((16, 16, 64, 128), BF),
            pltpu.VMEM((16, 16, 64, 128), BF),
            pltpu.VMEM((16, 64, 128), BF),
            pltpu.VMEM((16, 64, 128), BF),
            pltpu.VMEM((2, 16, 64, 128), BF),
            pltpu.VMEM((16, 64, 128), F32),
            pltpu.VMEM((16, 64, 128), F32),
            pltpu.VMEM((16, 32, 128), F32),
            pltpu.VMEM((64, 64), F32),
            dma((3, near)),
            dma((3, near)),
            dma((3, far)),
            dma((3, far)),
            dma((3, far)),
            dma((3, far)),
            dma((2,)),
            dma((2,)),
            dma((every,)),
            dma((every,)),
            dma((every,)),
            dma((every,)),
            dma((4,)),
        ],
        compiler_params=pltpu.CompilerParams(
            collective_id=0, has_side_effects=True, vmem_limit_bytes=60 << 20
        ),
    )(inv, kt, ot, vd, vv)


def body(tensor_blocks, occupied, virtual, slot_block, pair_kept, block_funcs):
    slab = block_funcs.shape[0]
    region = occupied.shape[0]
    width = occupied.shape[2]
    grp, tp = lax.axis_index("grp"), lax.axis_index("tp")
    regions = lax.axis_size("grp")
    first = grp * region
    slot_cols = slot_block[0]
    index = jnp.arange(region, dtype=jnp.int32)
    inv = jnp.sum(jnp.where(slot_cols[None, :] == index[:, None], index[None, :], 0), axis=1)
    local = jnp.sum(jnp.where(index == tp, slot_cols, 0))
    col = first + local

    zeros2 = jnp.zeros((2,), jnp.int32)
    funcs = lax.dynamic_slice_in_dim(
        jnp.concatenate([zeros2, block_funcs, zeros2]), first, region + 4
    )
    kept = lax.dynamic_slice_in_dim(
        jnp.concatenate([zeros2, pair_kept, zeros2]), first, region + 4
    )
    lane = jnp.arange(width, dtype=jnp.int32)

    up = [(i, i + 1) for i in range(regions - 1)]
    down = [(b, a) for a, b in up]
    low = lax.ppermute(occupied[region - 1, 1:3], "grp", up)
    high = lax.ppermute(occupied[0, 0:2], "grp", down)
    before = lax.dynamic_index_in_dim(occupied, jnp.maximum(local - 1, 0), 0, keepdims=False)
    here = lax.dynamic_index_in_dim(occupied, local, 0, keepdims=False)
    after = lax.dynamic_index_in_dim(occupied, jnp.minimum(local + 1, region - 1), 0, keepdims=False)
    before = jnp.where(local == 0, low, before[1:3])
    after = jnp.where(local == region - 1, high, after[0:2])
    none = jnp.zeros((1, width, width), occupied.dtype)
    blocks = jnp.stack(
        [
            jnp.concatenate([before, none]),
            here,
            jnp.concatenate([none, after]),
        ]
    )
    around = lax.dynamic_slice_in_dim(funcs, local + 1, 3)
    bonds = lax.dynamic_slice_in_dim(kept, local + 1, 2)
    pair_ok = jnp.stack([bonds[0] == 1, jnp.bool_(True), bonds[1] == 1])
    row_ok = (lane[None, :] < around[:, None]) & pair_ok[:, None]
    col_ok = lane[None, :] < around[:, None]
    keep = col_ok[:, None, None, :] & row_ok[None, :, :, None]
    blocks = jnp.where(keep, blocks, jnp.zeros_like(blocks))
    ot = jnp.transpose(blocks, (0, 3, 1, 2)).reshape(3 * width, 3 * width)

    own = lax.dynamic_index_in_dim(virtual, local, 0, keepdims=False)[1]
    own_ok = (lane[:, None] < around[1]) & (lane[None, :] < around[1])
    vd = jnp.where(
        own_ok[None] & pair_ok[:, None, None], own[None], jnp.zeros((3, width, width), own.dtype)
    )

    plain = lax.rem(tp // SIDE + lax.rem(tp, SIDE), 2) == 1
    row_lo = jnp.where(plain | (kept[1 : region + 1] == 1), funcs[1 : region + 1], 0)
    row_hi = jnp.where(plain | (kept[2 : region + 2] == 1), funcs[3 : region + 3], 0)
    limits = jnp.stack([row_lo, row_hi], axis=1)
    pair = jnp.stack([virtual[:, 0], virtual[:, 2]], axis=1)
    live = (lane[None, None, :, None] < limits[:, :, None, None]) & (
        lane[None, None, None, :] < funcs[2 : region + 2, None, None, None]
    )
    vv = jnp.where(live, pair, jnp.zeros_like(pair))

    return fused(inv, tensor_blocks[0], ot, vd, vv)[None]


def solution(mesh):
    placed = (
        P(("grp", "tp"), None, None, None, None),
        P("grp", None, None, None),
        P("grp", None, None, None),
        P("grp", None),
        P(),
        P(),
    )
    return jax.shard_map(
        body,
        mesh=mesh,
        in_specs=placed,
        out_specs=P(("grp", "tp"), None, None, None),
        check_vma=False,
    )
```

profile of v0, /device:TPU:113, one launch (start us, length us, event | category | flops | bytes accessed | tf_op | source)
XLA Modules:
  0.0 224.1 jit_solution(7313300581193245888)
XLA Ops:
  0.0 0.9 slice_bitcast_fusion.1
  0.9 5.3 %collective-permute-start = (bf16[2,128,128]{2,1,0:T(8,128)(2,1)S(1)}, bf16[2,128,128]{2,1,0:T(8,128)(2,1)S(1)}, u32[]{:S(2)}, u32[]{:S(2)}) collective-permute-start(bf16[2,128,128]{2,1,0:T(8,128)(2,1)S(1)} %get-tuple-element.9), channel_id=1, source_target_pairs={{0,16},{16,32},{32,48},{48,64},{64,80},{80,96},{96,112},{112,128},... | collective-permute-start | bytes 196616 | tf_op jit(solution)/shard_map/ppermute | solution.py:350
  6.2 1.9 collective-permute-start.1
  8.2 1.3 fusion.3
  13.4 0.8 pad_add_fusion.1
  14.4 0.1 copy.12
  14.5 0.1 iota_compare_fusion
  14.6 1.3 fusion.6
  16.7 0.7 fusion.7
  18.7 0.6 slice.61
  19.3 0.1 pad_add_fusion.4
  20.1 0.9 constant_dynamic-slice_fusion
  21.0 0.6 iota_compare_fusion.4
  21.6 0.1 broadcast_and_fusion
  21.6 0.8 dynamic-slice_bitcast_fusion.2
  22.4 0.7 and_select_fusion.2.vd
  23.1 1.5 and_select_fusion.vv
  24.6 0.6 select_reduce_fusion.inv
  25.3 0.9 fusion.2
  26.2 0.2 fusion
  26.4 0.2 copy.11
  26.6 0.8 copy.15
  27.4 195.1 %shard_map.64 = f32[5,64,64]{2,1,0:T(8,128)} custom-call(s32[16]{0:T(128)} %select_reduce_fusion.inv, bf16[3,128,64,128]{3,2,1,0:T(8,128)(2,1)} %bitcast.34, bf16[384,384]{1,0:T(8,128)(2,1)} %bitcast.36, bf16[3,128,128]{2,1,0:T(8,128)(2,1)} %and_select_fusion.2.vd, bf16[16,2,128,128]{3,2,1,0:T(8,128)(2,1)} %and_select_fusion.vv), custom_call_target="tpu_custom_call" | custom-call | tf_op jit(solution)/shard_map/pallas_call | solution.py:279
  222.5 1.6 copy.17
  (14 shorter events, 0.6 us)
Async XLA Ops:
  0.9 24.4 %collective-permute-start = (bf16[2,128,128]{2,1,0:T(8,128)(2,1)S(1)}, bf16[2,128,128]{2,1,0:T(8,128)(2,1)S(1)}, u32[]{:S(2)}, u32[]{:S(2)}) collective-permute-start(bf16[2,128,128]{2,1,0:T(8,128)(2,1)S(1)} %get-tuple-element.9), channel_id=1, source_target_pairs={{0,16},{16,32},{32,48},{48,64},{64,80},{80,96},{96,112},{112,128},... | collective-permute-start | bytes 196616 | tf_op jit(solution)/shard_map/ppermute | solution.py:350
  6.2 19.1 %collective-permute-start.1 = (bf16[2,128,128]{2,1,0:T(8,128)(2,1)S(1)}, bf16[2,128,128]{2,1,0:T(8,128)(2,1)S(1)}, u32[]{:S(2)}, u32[]{:S(2)}) collective-permute-start(bf16[2,128,128]{2,1,0:T(8,128)(2,1)S(1)} %get-tuple-element.10), channel_id=1, source_target_pairs={{16,0},{32,16},{48,32},{64,48},{80,64},{96,80},{112,96},{128,112},... | collective-permute-start | bytes 196616 | tf_op jit(solution)/shard_map/ppermute | solution.py:351
  15.9 8.7 %copy-start = (s32[1,16]{1,0:T(1,128)S(1)}, s32[1,16]{1,0:T(1,128)}, u32[]{:S(2)}) copy-start(s32[1,16]{1,0:T(1,128)} %param.9) | copy-start | bytes 196
where the time goes:
time: 226 us; the launch traced here: 224 us
  Pallas kernels  195 us (86%)
  local copies, waits for them, and re-layouts  8.08 us (4%)
  starting transfers between devices  7.24 us (3%)
  other arithmetic  7.04 us (3%)
  between operations  6.63 us (3%)
    pallas_call x1, Pallas kernels, fused(): pl.pallas_call(kernel, out_shape=jax.ShapeDtypeStruct((5, 64, 64), F32),...  195 us
    ppermute x1, starting transfers between devices, body(): low = lax.ppermute(occupied[region - 1, 1:3], 'grp', up)  5.32 us
  transfers between devices with their start and end apart: 2, of which 0 were waited for; matrix products, arithmetic and copies ran while one was open for 5% of the time, Pallas kernels for 0%

commit v1 on v0

v1 whole, which is shorter than its diff:
```python
import jax
import jax.numpy as jnp
from jax import lax
from jax.experimental import pallas as pl
from jax.experimental.pallas import tpu as pltpu
from jax.sharding import PartitionSpec as P

MESH = pl.DeviceIdType.MESH
BF = jnp.bfloat16
F32 = jnp.float32
SIDE = 4

NEAR = [(dx, dy) for dy in (-1, 0, 1) for dx in (-1, 0, 1) if (dx, dy) != (0, 0)]
FAR = [(2, 0), (0, 2), (2, 1), (2, -1), (1, 2), (-1, 2), (2, 2)]
RELAY = []
for _dx, _dy in FAR:
    for _half, _sign in enumerate((1, -1)):
        _first = (_sign if _dx == 2 else _dx, _sign if _dy == 2 else _dy)
        RELAY.append((_first, (_dx - _first[0], _dy - _first[1]), _half))
ALL = NEAR + FAR
AUX = ((0, 48), (48, 16))


def place(dx, dy):
    me = lax.axis_index("tp")
    x = lax.rem(lax.rem(me, SIDE) + (dx + SIDE), SIDE)
    y = lax.rem(me // SIDE + (dy + SIDE), SIDE)
    return y * SIDE + x


def slice_of(tp):
    x, y = lax.rem(tp, SIDE), tp // SIDE
    return y * 2 + x // 2, lax.rem(x + y, 2)


def lanes(x):
    return jnp.concatenate([x[i] for i in range(x.shape[0])], axis=1)


def dot_nt(a, b):
    return lax.dot_general(a, b, (((1,), (1,)), ((), ())), preferred_element_type=F32)


def masked(block, row_limit, col_limit):
    row = lax.broadcasted_iota(jnp.int32, block.shape, 0)
    col = lax.broadcasted_iota(jnp.int32, block.shape, 1)
    return jnp.where((row < row_limit) & (col < col_limit), block.astype(F32), 0.0)


def kernel(
    slot_ref, kept_ref, funcs_ref, tensor, occupied, virtual, out,
    inv, oe, ve, ot, vd, kh, k32, h32, r01, r2a, r2b, rb, rba, rbb, zd, zu, ed, eu, es, pt, fin, dg, acc,
    near_s, near_r, one_s, one_r, two_s, two_r, edge_s, edge_r, fin_s, fin_r, dg_s, dg_r,
    halo_s, halo_r, loc,
):
    me = lax.axis_index("tp")
    grp = lax.axis_index("grp")
    regions = lax.axis_size("grp")
    rows = 16
    kind = slice_of(me)[1]

    def dev(dx, dy):
        return (grp, place(dx, dy))

    def grp_at(step):
        return (lax.rem(grp + step + regions, regions), me)

    kt = tensor.at[0]
    region = occupied.shape[0]
    slab = funcs_ref.shape[0]
    first = grp * region
    loads = [
        pltpu.make_async_copy(occupied, oe.at[pl.ds(1, region)], loc.at[5]),
        pltpu.make_async_copy(kt, kh.at[pl.ds(0, 3)], loc.at[4]),
        pltpu.make_async_copy(virtual, ve, loc.at[6]),
    ]
    for c in loads:
        c.start()

    barrier = pltpu.get_barrier_semaphore()
    for dx, dy in ALL:
        pl.semaphore_signal(barrier, inc=1, device_id=dev(dx, dy), device_id_type=MESH)
    for step in (1, -1):
        pl.semaphore_signal(barrier, inc=1, device_id=grp_at(step), device_id_type=MESH)
    pl.semaphore_wait(barrier, len(ALL) + 2)

    def landing(slot, origin):
        return (r01.at[0, origin], r01.at[1, origin], r2a.at[origin], r2b.at[origin])[slot]

    def relayed(slot, i):
        return (rb.at[0, i], rb.at[1, i], rba.at[i], rbb.at[i])[slot]

    def source(slot, target, start, count):
        u, v = slice_of(target)
        part = pl.ds(u * rows + start, count)
        if slot == 0:
            return kt.at[v, part]
        if slot == 1:
            return kh.at[2 + 3 * v, part]
        return kh.at[4 - v, part, pl.ds(*AUX[slot - 2])]

    def send_far(slot):
        firsts = []
        for i, (hop, second, half) in enumerate(RELAY):
            target = place(hop[0] + second[0], hop[1] + second[1])
            c = pltpu.make_async_remote_copy(
                src_ref=source(slot, target, half * 8, 8),
                dst_ref=relayed(slot, i),
                send_sem=one_s.at[slot, i],
                recv_sem=one_r.at[slot, i],
                device_id=dev(*hop),
                device_id_type=MESH,
            )
            c.start()
            firsts.append(c)
        return firsts

    def send_near(slot):
        nears = []
        for i, (dx, dy) in enumerate(NEAR):
            c = pltpu.make_async_remote_copy(
                src_ref=source(slot, place(dx, dy), 0, rows),
                dst_ref=landing(slot, me),
                send_sem=near_s.at[slot, i],
                recv_sem=near_r.at[slot, i],
                device_id=dev(dx, dy),
                device_id_type=MESH,
            )
            c.start()
            nears.append(c)
        own = pltpu.make_async_copy(source(slot, me, 0, rows), landing(slot, me), loc.at[slot])
        own.start()
        return nears, own

    def forward(slot, firsts):
        seconds = []
        for i, (hop, second, half) in enumerate(RELAY):
            firsts[i].wait_recv()
            c = pltpu.make_async_remote_copy(
                src_ref=relayed(slot, i),
                dst_ref=landing(slot, place(-hop[0], -hop[1])).at[pl.ds(half * 8, 8)],
                send_sem=two_s.at[slot, i],
                recv_sem=two_r.at[slot, i],
                device_id=dev(*second),
                device_id_type=MESH,
            )
            c.start()
            seconds.append(c)
        return seconds

    def arrive(nears, own, seconds):
        own.wait()
        for c in nears + seconds:
            c.wait_recv()

    firsts0 = send_far(0)
    halos = []
    for i, (step, src, dst) in enumerate(
        (
            (1, occupied.at[region - 1, pl.ds(1, 2)], oe.at[0, pl.ds(1, 2)]),
            (-1, occupied.at[0, pl.ds(0, 2)], oe.at[region + 1, pl.ds(0, 2)]),
        )
    ):
        c = pltpu.make_async_remote_copy(
            src_ref=src,
            dst_ref=dst,
            send_sem=halo_s.at[i],
            recv_sem=halo_r.at[i],
            device_id=grp_at(step),
            device_id_type=MESH,
        )
        c.start()
        halos.append(c)
    oe[0, 0] = jnp.zeros(oe.shape[2:], BF)
    oe[region + 1, 2] = jnp.zeros(oe.shape[2:], BF)

    def funcs(col):
        inside = (col >= 0) & (col < slab)
        return jnp.where(inside, funcs_ref[jnp.clip(col, 0, slab - 1)], 0)

    def bond(col):
        inside = (col >= 0) & (col < slab)
        return jnp.where(inside, kept_ref[jnp.clip(col, 0, slab - 1)], 0)

    def find(j, _):
        at = 0
        for k in range(region):
            at = jnp.where(slot_ref[0, k] == j, k, at)
        inv[j] = at
        return 0

    lax.fori_loop(0, region, find, 0)
    local = slot_ref[0, me]
    own_col = first + local
    around = [funcs(own_col - 1), funcs(own_col), funcs(own_col + 1)]
    rows_ok = [
        jnp.where(bond(own_col - 1) == 1, around[0], 0),
        around[1],
        jnp.where(bond(own_col) == 1, around[2], 0),
    ]
    loads[0].wait()
    for c in halos:
        c.wait_recv()
    for e in range(3):
        for d in range(3):
            if abs(d - e) > 1:
                block = jnp.zeros((128, 128), BF)
            else:
                block = masked(oe[local + e, d - e + 1], rows_ok[d], around[e]).T.astype(BF)
            ot[e * 128 : (e + 1) * 128, d * 128 : (d + 1) * 128] = block
    loads[1].wait()

    def half_chunk(i, _):
        cut = pl.ds(pl.multiple_of(i * 16, 16), 16)
        for d in range(3):
            k32[pl.ds(d * 2048, 2048), :] = kh[d, :, cut, :].reshape(2048, 128).astype(F32)
        for q in range(0, 16, 2):
            two = [k32[pl.ds(q + s, 384, stride=16), :] for s in range(2)]
            res = jnp.dot(
                ot[...], jnp.concatenate(two, axis=1).astype(BF), preferred_element_type=F32
            )
            for s in range(2):
                h32[pl.ds(q + s, 384, stride=16), :] = res[:, s * 128 : (s + 1) * 128]
        for e in range(3):
            kh[3 + e, :, cut, :] = h32[pl.ds(e * 2048, 2048), :].reshape(128, 16, 128).astype(BF)
        return 0

    lax.fori_loop(0, 4, half_chunk, 0)

    firsts1 = send_far(1)
    firsts2 = send_far(2)
    firsts3 = send_far(3)
    seconds0 = forward(0, firsts0)
    seconds1 = forward(1, firsts1)
    nears0, own0 = send_near(0)
    nears1, own1 = send_near(1)
    seconds2 = forward(2, firsts2)
    nears2, own2 = send_near(2)
    seconds3 = forward(3, firsts3)
    nears3, own3 = send_near(3)
    loads[2].wait()
    for e in range(3):
        allowed = jnp.where(rows_ok[e] > 0, around[1], 0)
        vd[e] = masked(ve[local, 1], allowed, around[1]).astype(BF)
    acc[...] = jnp.zeros_like(acc)

    def own_part(i, _):
        e, cut = i // 8, pl.ds(lax.rem(i, 8) * 16, 16)
        z = jnp.dot(kh[e, cut].reshape(1024, 128), vd[e], preferred_element_type=F32)
        acc[...] += dot_nt(lanes(kh[3 + e, cut]), lanes(z.astype(BF).reshape(16, 64, 128)))
        return 0

    lax.fori_loop(0, 24, own_part, 0)
    dg[me] = jnp.concatenate([acc[:32], acc[32:]], axis=1)
    shares = []
    for i, (dx, dy) in enumerate(ALL):
        c = pltpu.make_async_remote_copy(
            src_ref=dg.at[me],
            dst_ref=dg.at[me],
            send_sem=dg_s.at[i],
            recv_sem=dg_r.at[i],
            device_id=dev(dx, dy),
            device_id_type=MESH,
        )
        c.start()
        shares.append(c)
    arrive(nears0, own0, seconds0)
    arrive(nears1, own1, seconds1)

    es[0] = r01[0, inv[0]]
    es[1] = r01[1 - kind, inv[15]]
    edges = []
    for i, (step, dst) in enumerate(((-1, ed), (1, eu))):
        c = pltpu.make_async_remote_copy(
            src_ref=es.at[i],
            dst_ref=dst,
            send_sem=edge_s.at[i],
            recv_sem=edge_r.at[i],
            device_id=grp_at(step),
            device_id_type=MESH,
        )
        c.start()
        edges.append(c)

    def times(block, j, side):
        col = first + j
        beside = funcs(col + side - 1)
        allowed = jnp.where((kind == 1) | (bond(col + side // 2 - 1) == 1), beside, 0)
        v = masked(ve[j, side], allowed, funcs(col)).astype(BF)
        z = jnp.dot(block.reshape(1024, 128), v, preferred_element_type=F32)
        return z.astype(BF).reshape(16, 64, 128)

    def other_part(j, _):
        zd[j] = times(r01[0, inv[j + 1]], j, 2)
        zu[j + 1] = times(r01[1 - kind, inv[j]], j + 1, 0)
        return 0

    lax.fori_loop(0, 15, other_part, 0)
    for c in edges:
        c.wait_recv()
    zd[15] = times(ed[...], 15, 2)
    zu[0] = times(eu[...], 0, 0)

    sums = []

    def finish(part, landed):
        start, count = AUX[part]
        cut = pl.ds(start, count)

        @pl.when(kind == 0)
        def _():
            def column(j, _):
                half = lanes(landed[inv[j]])
                pt[j, cut] = jnp.concatenate(
                    [dot_nt(half, lanes(zu[j])), dot_nt(half, lanes(zd[j]))], axis=1
                )
                return 0

            lax.fori_loop(0, 16, column, 0)

        @pl.when(kind == 1)
        def _():
            def column(j, _):
                pt[j, cut] = jnp.concatenate(
                    [
                        dot_nt(lanes(landed[inv[j]]), lanes(zu[j])),
                        dot_nt(lanes(r01[1, inv[j], :, cut]), lanes(zd[j])),
                    ],
                    axis=1,
                )
                return 0

            lax.fori_loop(0, 16, column, 0)

        for i, (dx, dy) in enumerate(ALL):
            c = pltpu.make_async_remote_copy(
                src_ref=pt.at[place(dx, dy), cut],
                dst_ref=fin.at[me, cut],
                send_sem=fin_s.at[part, i],
                recv_sem=fin_r.at[part, i],
                device_id=dev(dx, dy),
                device_id_type=MESH,
            )
            c.start()
            sums.append(c)

    arrive(nears2, own2, seconds2)
    finish(0, r2a)
    arrive(nears3, own3, seconds3)
    finish(1, r2b)
    fin[me] = pt[me]
    for c in shares + sums:
        c.wait_recv()
    scale = 1.0 / 128
    total = fin[0]
    for k in range(1, 16):
        total = total + fin[k]
    total = total * scale
    mid = dg[inv[me]] * scale
    out[0, 0] = jnp.zeros((64, 64), F32)
    out[0, 1] = total[:, :64]
    out[0, 2] = jnp.concatenate([mid[:, :64], mid[:, 64:]], axis=0)
    out[0, 3] = total[:, 64:]
    out[0, 4] = jnp.zeros((64, 64), F32)

    for c in firsts0 + firsts1 + firsts2 + firsts3 + nears0 + nears1 + nears2 + nears3:
        c.wait_send()
    for c in seconds0 + seconds1 + seconds2 + seconds3 + halos + edges + shares + sums:
        c.wait_send()


def body(tensor_blocks, occupied, virtual, slot_block, pair_kept, block_funcs):
    dma = pltpu.SemaphoreType.DMA
    smem = pl.BlockSpec(memory_space=pltpu.SMEM)
    hbm = pl.BlockSpec(memory_space=pl.ANY)
    near, far, every = len(NEAR), len(RELAY), len(ALL)
    return pl.pallas_call(
        kernel,
        out_shape=jax.ShapeDtypeStruct((1, 5, 64, 64), F32),
        in_specs=[smem, smem, smem, hbm, hbm, hbm],
        out_specs=pl.BlockSpec(memory_space=pltpu.VMEM),
        scratch_shapes=[
            pltpu.SMEM((16,), jnp.int32),
            pltpu.VMEM((18, 3, 128, 128), BF),
            pltpu.VMEM((16, 3, 128, 128), BF),
            pltpu.VMEM((384, 384), BF),
            pltpu.VMEM((3, 128, 128), BF),
            pltpu.VMEM((6, 128, 64, 128), BF),
            pltpu.VMEM((6144, 128), F32),
            pltpu.VMEM((6144, 128), F32),
            pltpu.VMEM((2, 16, 16, 64, 128), BF),
            pltpu.VMEM((16, 16, AUX[0][1], 128), BF),
            pltpu.VMEM((16, 16, AUX[1][1], 128), BF),
            pltpu.VMEM((2, far, 8, 64, 128), BF),
            pltpu.VMEM((far, 8, AUX[0][1], 128), BF),
            pltpu.VMEM((far, 8, AUX[1][1], 128), BF),
            pltpu.VMEM((16, 16, 64, 128), BF),
            pltpu.VMEM((16, 16, 64, 128), BF),
            pltpu.VMEM((16, 64, 128), BF),
            pltpu.VMEM((16, 64, 128), BF),
            pltpu.VMEM((2, 16, 64, 128), BF),
            pltpu.VMEM((16, 64, 128), F32),
            pltpu.VMEM((16, 64, 128), F32),
            pltpu.VMEM((16, 32, 128), F32),
            pltpu.VMEM((64, 64), F32),
            dma((4, near)),
            dma((4, near)),
            dma((4, far)),
            dma((4, far)),
            dma((4, far)),
            dma((4, far)),
            dma((2,)),
            dma((2,)),
            dma((2, every)),
            dma((2, every)),
            dma((every,)),
            dma((every,)),
            dma((2,)),
            dma((2,)),
            dma((7,)),
        ],
        compiler_params=pltpu.CompilerParams(
            collective_id=0, has_side_effects=True, vmem_limit_bytes=60 << 20
        ),
    )(slot_block, pair_kept, block_funcs, tensor_blocks, occupied, virtual)


def solution(mesh):
    placed = (
        P(("grp", "tp"), None, None, None, None),
        P("grp", None, None, None),
        P("grp", None, None, None),
        P("grp", None),
        P(),
        P(),
    )
    return jax.shard_map(
        body,
        mesh=mesh,
        in_specs=placed,
        out_specs=P(("grp", "tp"), None, None, None),
        check_vma=False,
    )
```

time: 226 us -> 180 us (0.80)
  Pallas kernels: 195 us -> 179 us
  starting transfers between devices: 7.24 us -> 0 us
  other arithmetic: 7.04 us -> 0 us
  between operations: 6.63 us -> 0.01 us
  local copies, waits for them, and re-layouts: 8.08 us -> 1.59 us
    pallas_call x1, Pallas kernels: 195 us -> 179 us  [body(): pl.pallas_call(kernel, out_shape=jax.ShapeDtypeStruct((1, 5, 64, 64), F32...]
    ppermute x2 -> x0, starting transfers between devices: 7.24 us -> none  [the longest x1 5.32 us: body(): low = lax.ppermute(occupied[region - 1, 1:3], 'grp', up)]
    select_n x3 -> x0, other arithmetic: 3.11 us -> none  [the longest x1 1.48 us: body(): vv = jnp.where(live, pair, jnp.zeros_like(pair))]
    slice x3 -> x0, local copies, waits for them, and re-layouts: 2.52 us -> none  [the longest x1 1.27 us: body(): pair = jnp.stack([virtual[:, 0], virtual[:, 2]], axis=1)]
  transfers between devices with their start and end apart: 2 -> 0, of which waited for: 0 -> 0; matrix products, arithmetic and copies ran while one was open for 5% -> 0% of each run, Pallas kernels for 0% -> 0%
where the time goes in v1:
time: 180 us
  Pallas kernels  179 us (99%)
    pallas_call x1, Pallas kernels, body(): pl.pallas_call(kernel, out_shape=jax.ShapeDtypeStruct((1, 5, 64, 64), F32...  179 us

profile of v1, /device:TPU:113, one launch (start us, length us, event | category | flops | bytes accessed | tf_op | source)
XLA Modules:
  0.0 180.2 jit_solution(9356619660766100560)
XLA Ops:
  0.0 178.6 %shard_map.64 = f32[1,5,64,64]{3,2,1,0:T(8,128)} custom-call(s32[1,16]{1,0:T(1,128)} %slot_ref.1, s32[256]{0:T(256)} %kept_ref.1, s32[256]{0:T(256)} %funcs_ref.1, bf16[1,3,128,64,128]{4,3,2,1,0:T(8,128)(2,1)} %tensor.1, bf16[16,3,128,128]{3,2,1,0:T(8,128)(2,1)} %occupied.1, bf16[16,3,128,128]{3,2,1,0:T(8,128)(2,1)} %virtual.1), custom_call_target="tpu_custom_call" | custom-call | tf_op jit(solution)/shard_map/pallas_call | solution.py:377
  178.6 1.6 copy.8

commit v2 on v1

--- a/solution.py
+++ b/solution.py
@@ -51,7 +51,7 @@
     slot_ref, kept_ref, funcs_ref, tensor, occupied, virtual, out,
     inv, oe, ve, ot, vd, kh, k32, h32, r01, r2a, r2b, rb, rba, rbb, zd, zu, ed, eu, es, pt, fin, dg, acc,
     near_s, near_r, one_s, one_r, two_s, two_r, edge_s, edge_r, fin_s, fin_r, dg_s, dg_r,
-    halo_s, halo_r, loc,
+    halo_s, halo_r, loc, ready,
 ):
     me = lax.axis_index("tp")
     grp = lax.axis_index("grp")
@@ -80,9 +80,9 @@
     barrier = pltpu.get_barrier_semaphore()
     for dx, dy in ALL:
         pl.semaphore_signal(barrier, inc=1, device_id=dev(dx, dy), device_id_type=MESH)
-    for step in (1, -1):
-        pl.semaphore_signal(barrier, inc=1, device_id=grp_at(step), device_id_type=MESH)
-    pl.semaphore_wait(barrier, len(ALL) + 2)
+    pl.semaphore_signal(barrier, inc=1, device_id=grp_at(1), device_id_type=MESH)
+    pl.semaphore_wait(barrier, len(ALL) + 1)
+    pl.semaphore_signal(ready, inc=1, device_id=grp_at(-1), device_id_type=MESH)
 
     def landing(slot, origin):
         return (r01.at[0, origin], r01.at[1, origin], r2a.at[origin], r2b.at[origin])[slot]
@@ -90,28 +90,33 @@
     def relayed(slot, i):
         return (rb.at[0, i], rb.at[1, i], rba.at[i], rbb.at[i])[slot]
 
-    def source(slot, target, start, count):
+    def source(slot, target, start, count, early=False):
         u, v = slice_of(target)
         part = pl.ds(u * rows + start, count)
         if slot == 0:
             return kt.at[v, part]
+        if slot == 1 and early:
+            return kt.at[2, part]
         if slot == 1:
             return kh.at[2 + 3 * v, part]
         return kh.at[4 - v, part, pl.ds(*AUX[slot - 2])]
 
-    def send_far(slot):
+    def send_far(slot, only=None):
         firsts = []
         for i, (hop, second, half) in enumerate(RELAY):
             target = place(hop[0] + second[0], hop[1] + second[1])
             c = pltpu.make_async_remote_copy(
-                src_ref=source(slot, target, half * 8, 8),
+                src_ref=source(slot, target, half * 8, 8, only == 0),
                 dst_ref=relayed(slot, i),
                 send_sem=one_s.at[slot, i],
                 recv_sem=one_r.at[slot, i],
                 device_id=dev(*hop),
                 device_id_type=MESH,
             )
-            c.start()
+            if only is None:
+                c.start()
+            else:
+                pl.when(slice_of(target)[1] == only)(c.start)
             firsts.append(c)
         return firsts
 
@@ -154,13 +159,36 @@
             c.wait_recv()
 
     firsts0 = send_far(0)
+    send_far(1, 0)
+    oe[0, 0] = jnp.zeros(oe.shape[2:], BF)
+    oe[region + 1, 2] = jnp.zeros(oe.shape[2:], BF)
+
+    def funcs(col):
+        inside = (col >= 0) & (col < slab)
+        return jnp.where(inside, funcs_ref[jnp.clip(col, 0, slab - 1)], 0)
+
+    def bond(col):
+        inside = (col >= 0) & (col < slab)
+        return jnp.where(inside, kept_ref[jnp.clip(col, 0, slab - 1)], 0)
+
+    def find(j, _):
+        at = 0
+        for k in range(region):
+            at = jnp.where(slot_ref[0, k] == j, k, at)
+        inv[j] = at
+        return 0
+
+    lax.fori_loop(0, region, find, 0)
+
     halos = []
     for i, (step, src, dst) in enumerate(
         (
+            (-1, occupied.at[0, pl.ds(0, 2)], oe.at[region + 1, pl.ds(0, 2)]),
             (1, occupied.at[region - 1, pl.ds(1, 2)], oe.at[0, pl.ds(1, 2)]),
-            (-1, occupied.at[0, pl.ds(0, 2)], oe.at[region + 1, pl.ds(0, 2)]),
         )
     ):
+        if step == 1:
+            pl.semaphore_wait(ready, 1)
         c = pltpu.make_async_remote_copy(
             src_ref=src,
             dst_ref=dst,
@@ -171,25 +199,7 @@
         )
         c.start()
         halos.append(c)
-    oe[0, 0] = jnp.zeros(oe.shape[2:], BF)
-    oe[region + 1, 2] = jnp.zeros(oe.shape[2:], BF)
-
-    def funcs(col):
-        inside = (col >= 0) & (col < slab)
-        return jnp.where(inside, funcs_ref[jnp.clip(col, 0, slab - 1)], 0)
-
-    def bond(col):
-        inside = (col >= 0) & (col < slab)
-        return jnp.where(inside, kept_ref[jnp.clip(col, 0, slab - 1)], 0)
-
-    def find(j, _):
-        at = 0
-        for k in range(region):
-            at = jnp.where(slot_ref[0, k] == j, k, at)
-        inv[j] = at
-        return 0
-
-    lax.fori_loop(0, region, find, 0)
+
     local = slot_ref[0, me]
     own_col = first + local
     around = [funcs(own_col - 1), funcs(own_col), funcs(own_col + 1)]
@@ -227,7 +237,7 @@
 
     lax.fori_loop(0, 4, half_chunk, 0)
 
-    firsts1 = send_far(1)
+    firsts1 = send_far(1, 1)
     firsts2 = send_far(2)
     firsts3 = send_far(3)
     seconds0 = forward(0, firsts0)
@@ -418,6 +428,7 @@
             dma((2,)),
             dma((2,)),
             dma((7,)),
+            pltpu.SemaphoreType.REGULAR,
         ],
         compiler_params=pltpu.CompilerParams(
             collective_id=0, has_side_effects=True, vmem_limit_bytes=60 << 20

time: 180 us -> 172 us (0.956); the launches traced: 180 us -> 169 us
  Pallas kernels: 179 us -> 168 us
    pallas_call x1, Pallas kernels: 179 us -> 168 us  [body(): pl.pallas_call(kernel, out_shape=jax.ShapeDtypeStruct((1, 5, 64, 64), F32...]
where the time goes in v2:
time: 172 us; the launch traced here: 169 us
  Pallas kernels  168 us (98%)
    pallas_call x1, Pallas kernels, body(): pl.pallas_call(kernel, out_shape=jax.ShapeDtypeStruct((1, 5, 64, 64), F32...  168 us

profile of v2, /device:TPU:113, one launch (start us, length us, event | category | flops | bytes accessed | tf_op | source)
XLA Modules:
  0.0 169.1 jit_solution(3762762550980497601)
XLA Ops:
  0.0 167.5 %shard_map.64 = f32[1,5,64,64]{3,2,1,0:T(8,128)} custom-call(s32[1,16]{1,0:T(1,128)} %slot_ref.1, s32[256]{0:T(256)} %kept_ref.1, s32[256]{0:T(256)} %funcs_ref.1, bf16[1,3,128,64,128]{4,3,2,1,0:T(8,128)(2,1)} %tensor.1, bf16[16,3,128,128]{3,2,1,0:T(8,128)(2,1)} %occupied.1, bf16[16,3,128,128]{3,2,1,0:T(8,128)(2,1)} %virtual.1), custom_call_target="tpu_custom_call" | custom-call | tf_op jit(solution)/shard_map/pallas_call | solution.py:387
  167.5 1.6 copy.8

commit v3 on v2

--- a/solution.py
+++ b/solution.py
@@ -10,7 +10,7 @@
 F32 = jnp.float32
 SIDE = 4
 
-NEAR = [(dx, dy) for dy in (-1, 0, 1) for dx in (-1, 0, 1) if (dx, dy) != (0, 0)]
+NEAR = [(-1, -1), (1, -1), (-1, 1), (1, 1), (-1, 0), (1, 0), (0, -1), (0, 1)]
 FAR = [(2, 0), (0, 2), (2, 1), (2, -1), (1, 2), (-1, 2), (2, 2)]
 RELAY = []
 for _dx, _dy in FAR:
@@ -78,10 +78,10 @@
         c.start()
 
     barrier = pltpu.get_barrier_semaphore()
-    for dx, dy in ALL:
+    for dx, dy in NEAR:
         pl.semaphore_signal(barrier, inc=1, device_id=dev(dx, dy), device_id_type=MESH)
     pl.semaphore_signal(barrier, inc=1, device_id=grp_at(1), device_id_type=MESH)
-    pl.semaphore_wait(barrier, len(ALL) + 1)
+    pl.semaphore_wait(barrier, len(NEAR) + 1)
     pl.semaphore_signal(ready, inc=1, device_id=grp_at(-1), device_id_type=MESH)
 
     def landing(slot, origin):
@@ -262,6 +262,9 @@
 
     lax.fori_loop(0, 24, own_part, 0)
     dg[me] = jnp.concatenate([acc[:32], acc[32:]], axis=1)
+    arrive(nears0, own0, seconds0)
+    arrive(nears1, own1, seconds1)
+
     shares = []
     for i, (dx, dy) in enumerate(ALL):
         c = pltpu.make_async_remote_copy(
@@ -274,8 +277,6 @@
         )
         c.start()
         shares.append(c)
-    arrive(nears0, own0, seconds0)
-    arrive(nears1, own1, seconds1)
 
     es[0] = r01[0, inv[0]]
     es[1] = r01[1 - kind, inv[15]]

time: 172 us -> 171 us (level)
  no operation moved by 1% of the time
where the time goes in v3:
time: 171 us; the launch traced here: 168 us
  Pallas kernels  167 us (98%)
    pallas_call x1, Pallas kernels, body(): pl.pallas_call(kernel, out_shape=jax.ShapeDtypeStruct((1, 5, 64, 64), F32...  167 us

profile of v3, /device:TPU:113, one launch (start us, length us, event | category | flops | bytes accessed | tf_op | source)
XLA Modules:
  0.0 168.2 jit_solution(13230764914862767285)
XLA Ops:
  0.0 166.6 %shard_map.64 = f32[1,5,64,64]{3,2,1,0:T(8,128)} custom-call(s32[1,16]{1,0:T(1,128)} %slot_ref.1, s32[256]{0:T(256)} %kept_ref.1, s32[256]{0:T(256)} %funcs_ref.1, bf16[1,3,128,64,128]{4,3,2,1,0:T(8,128)(2,1)} %tensor.1, bf16[16,3,128,128]{3,2,1,0:T(8,128)(2,1)} %occupied.1, bf16[16,3,128,128]{3,2,1,0:T(8,128)(2,1)} %virtual.1), custom_call_target="tpu_custom_call" | custom-call | tf_op jit(solution)/shard_map/pallas_call | solution.py:388
  166.6 1.6 copy.8

commit v4 on v3

--- a/solution.py
+++ b/solution.py
@@ -10,7 +10,7 @@
 F32 = jnp.float32
 SIDE = 4
 
-NEAR = [(-1, -1), (1, -1), (-1, 1), (1, 1), (-1, 0), (1, 0), (0, -1), (0, 1)]
+NEAR = [(-1, -1), (1, 1), (1, -1), (-1, 1), (1, 0), (-1, 0), (0, 1), (0, -1)]
 FAR = [(2, 0), (0, 2), (2, 1), (2, -1), (1, 2), (-1, 2), (2, 2)]
 RELAY = []
 for _dx, _dy in FAR:

time: 171 us -> 167 us (0.977)
  the two profiles are of different devices: /device:TPU:113 before, /device:TPU:6 now
where the time goes in v4:
time: 167 us
  Pallas kernels  165 us (99%)
    pallas_call x1, Pallas kernels, body(): pl.pallas_call(kernel, out_shape=jax.ShapeDtypeStruct((1, 5, 64, 64), F32...  165 us

profile of v4, /device:TPU:6, one launch (start us, length us, event | category | flops | bytes accessed | tf_op | source)
XLA Modules:
  0.0 167.0 jit_solution(1275773730060374530)
XLA Ops:
  0.0 165.4 %shard_map.64 = f32[1,5,64,64]{3,2,1,0:T(8,128)} custom-call(s32[1,16]{1,0:T(1,128)} %slot_ref.1, s32[256]{0:T(256)} %kept_ref.1, s32[256]{0:T(256)} %funcs_ref.1, bf16[1,3,128,64,128]{4,3,2,1,0:T(8,128)(2,1)} %tensor.1, bf16[16,3,128,128]{3,2,1,0:T(8,128)(2,1)} %occupied.1, bf16[16,3,128,128]{3,2,1,0:T(8,128)(2,1)} %virtual.1), custom_call_target="tpu_custom_call" | custom-call | tf_op jit(solution)/shard_map/pallas_call | solution.py:388
  165.4 1.6 copy.8

commit v5 on v4

--- a/solution.py
+++ b/solution.py
@@ -10,7 +10,7 @@
 F32 = jnp.float32
 SIDE = 4
 
-NEAR = [(-1, -1), (1, 1), (1, -1), (-1, 1), (1, 0), (-1, 0), (0, 1), (0, -1)]
+NEAR = [(-1, -1), (1, 1), (1, -1), (-1, 1), (0, 1), (0, -1), (1, 0), (-1, 0)]
 FAR = [(2, 0), (0, 2), (2, 1), (2, -1), (1, 2), (-1, 2), (2, 2)]
 RELAY = []
 for _dx, _dy in FAR:

time: 167 us -> 167 us (level)
  no operation moved by 1% of the time
where the time goes in v5:
time: 167 us
  Pallas kernels  165 us (99%)
    pallas_call x1, Pallas kernels, body(): pl.pallas_call(kernel, out_shape=jax.ShapeDtypeStruct((1, 5, 64, 64), F32...  165 us

profile of v5, /device:TPU:6, one launch (start us, length us, event | category | flops | bytes accessed | tf_op | source)
XLA Modules:
  0.0 167.0 jit_solution(6992365009954866013)
XLA Ops:
  0.0 165.4 %shard_map.64 = f32[1,5,64,64]{3,2,1,0:T(8,128)} custom-call(s32[1,16]{1,0:T(1,128)} %slot_ref.1, s32[256]{0:T(256)} %kept_ref.1, s32[256]{0:T(256)} %funcs_ref.1, bf16[1,3,128,64,128]{4,3,2,1,0:T(8,128)(2,1)} %tensor.1, bf16[16,3,128,128]{3,2,1,0:T(8,128)(2,1)} %occupied.1, bf16[16,3,128,128]{3,2,1,0:T(8,128)(2,1)} %virtual.1), custom_call_target="tpu_custom_call" | custom-call | tf_op jit(solution)/shard_map/pallas_call | solution.py:388
  165.4 1.6 copy.8
